TPU v7x, 512 devices: a whole 4x8x8 slice. The times are simulated.
512 devices in a mesh: tensor: 16 (over y_hi, x, core), context: 32 (over y_lo, z).
Axes of the slice: x: 4, y: 8 (y_hi: 2, y_lo: 4; y = y_hi * 4 + y_lo), z: 8, core: 2. Of those that a mesh axis runs over, the one named last changes fastest.
Arguments:
- values: bfloat16 [32768, 2048], P('context', 'tensor'), may hold values from -6 to 6
- long_filter: bfloat16 [32768, 2048], P('context', 'tensor'), may hold values from -0.03125 to 0.03125
- skip_gain: float32 [2048], P('tensor'), may hold values from -3 to 3
Outputs:
- layer_out: bfloat16 [32768, 2048], P('context', 'tensor')
All inputs are finite; a program needn't handle non-finite values.
Results may differ from a plain program's by a relative error of at most 0.011.
Values may be sent and summed in bfloat16 or wider, within the bound.
A program may use at most 64 MiB of HBM per device.

v0:
```python
import math

import jax
import jax.numpy as jnp
from jax import lax
from jax.sharding import PartitionSpec as P

F1 = 32


TWO_PI = 2.0 * math.pi


def dft_rows(length, sign_value):
    index_vals = jnp.arange(length, dtype=jnp.int32)
    product = index_vals[:, None] * index_vals[None, :] % length
    angles = TWO_PI / length * product.astype(jnp.float32)
    cosine = jnp.cos(angles)
    sine_part = sign_value * jnp.sin(angles)
    upper_rows = jnp.stack([cosine, -sine_part], axis=1)
    lower_rows = jnp.stack([sine_part, cosine], axis=1)
    return jnp.stack([upper_rows, lower_rows], axis=0).astype(jnp.bfloat16)


def column_rows(column_count, factor, sign_value):
    index_vals = jnp.arange(column_count, dtype=jnp.int32)
    product = index_vals[:, None] * index_vals[None, :] % (2 * column_count)
    angles = TWO_PI / (2 * column_count) * product.astype(jnp.float32)
    parity = 1.0 - 2.0 * (index_vals % 2).astype(jnp.float32)
    is_first = (index_vals == 0)[None, :]
    real_rows = jnp.where(is_first, 1.0, factor * jnp.cos(angles))
    imag_rows = jnp.where(is_first, parity[:, None], factor * sign_value * jnp.sin(angles))
    return jnp.stack([real_rows, imag_rows], axis=2).astype(jnp.bfloat16)


def complex_product(left_re, left_im, right_re, right_im):
    return (left_re * right_re - left_im * right_im, left_re * right_im + left_im * right_re)


def pack_lanes(real_part, imag_part, columns):
    half_lanes = real_part.shape[-1] // 2
    packed_re = jnp.concatenate([real_part[..., :half_lanes], imag_part[..., :half_lanes]], axis=-1)
    packed_im = jnp.concatenate([real_part[..., half_lanes:], imag_part[..., half_lanes:]], axis=-1)
    is_first = (columns == 0).reshape((-1,) + (1,) * (real_part.ndim - 1))
    return (jnp.where(is_first, packed_re, real_part), jnp.where(is_first, packed_im, imag_part))


def position_grid(a_start, a_count, b_count, b_total):
    a_vals = a_start + jnp.arange(a_count, dtype=jnp.int32)
    b_vals = jnp.arange(b_count, dtype=jnp.int32)
    return a_vals[:, None] * b_total + b_vals[None, :]


def column_twiddle(columns, position, lane_count, column_count, length, sign_value):
    lane_index = jnp.arange(lane_count, dtype=jnp.int32)
    column = columns.reshape(-1, 1, 1, 1)
    exponent = jnp.where(
        column == 0, jnp.where(lane_index >= lane_count // 2, column_count, 0), column
    )
    product = position[None, :, :, None] * exponent % length
    angles = sign_value * TWO_PI / length * product.astype(jnp.float32)
    return (jnp.cos(angles), jnp.sin(angles))


def row_twiddle(b_count, row_total, sign_value):
    s_vals = jnp.arange(F1, dtype=jnp.int32)
    b_vals = jnp.arange(b_count, dtype=jnp.int32)
    product = s_vals[:, None] * b_vals[None, :] % row_total
    angles = sign_value * TWO_PI / row_total * product.astype(jnp.float32)
    return (jnp.cos(angles)[None, :, :, None], jnp.sin(angles)[None, :, :, None])


def first_columns(blocks, table_a, columns, position, column_count, length):
    summed = jnp.einsum("cql,cabh->qlabh", table_a, blocks, preferred_element_type=jnp.float32)
    real_part, imag_part = pack_lanes(summed[:, 0], summed[:, 1], columns)
    cos_part, sin_part = column_twiddle(
        columns, position, blocks.shape[-1], column_count, length, -1.0
    )
    real_part, imag_part = complex_product(real_part, imag_part, cos_part, sin_part)
    return jnp.stack([real_part, imag_part], axis=1).astype(jnp.bfloat16)


def section_one(blocks, twiddle):
    summed = jnp.einsum(
        "osia,qiabh->qosbh", dft_rows(F1, -1.0), blocks, preferred_element_type=jnp.float32
    )
    real_part, imag_part = complex_product(summed[:, 0], summed[:, 1], twiddle[0], twiddle[1])
    return jnp.stack([real_part, imag_part], axis=1).astype(jnp.bfloat16)


def section_two(blocks):
    f_two = blocks.shape[3]
    summed = jnp.einsum(
        "otib,qisbh->qotsh", dft_rows(f_two, -1.0), blocks, preferred_element_type=jnp.float32
    )
    return summed.reshape(summed.shape[0], 2, f_two * F1, summed.shape[-1])


def back_two(blocks, twiddle):
    f_two = blocks.shape[2] // F1
    shaped = blocks.reshape(blocks.shape[0], 2, f_two, F1, blocks.shape[-1])
    summed = jnp.einsum(
        "obit,qitsh->qosbh", dft_rows(f_two, 1.0), shaped, preferred_element_type=jnp.float32
    )
    real_part, imag_part = complex_product(summed[:, 0], summed[:, 1], twiddle[0], twiddle[1])
    return jnp.stack([real_part, imag_part], axis=1).astype(jnp.bfloat16)


def back_one(blocks, columns, position, column_count, length):
    summed = jnp.einsum(
        "oais,qisbh->qoabh", dft_rows(F1, 1.0), blocks, preferred_element_type=jnp.float32
    )
    cos_part, sin_part = column_twiddle(
        columns, position, blocks.shape[-1], column_count, length, 1.0
    )
    real_part, imag_part = complex_product(summed[:, 0], summed[:, 1], cos_part, sin_part)
    return jnp.stack([real_part, imag_part], axis=1).astype(jnp.bfloat16)


def last_rows(blocks, table_b, columns, length):
    real_part, imag_part = pack_lanes(blocks[:, 0], blocks[:, 1], columns)
    packed = jnp.stack([real_part, imag_part], axis=1)
    summed = jnp.einsum("cql,qlabh->cabh", table_b, packed, preferred_element_type=jnp.float32)
    return (summed * (1.0 / length)).astype(jnp.bfloat16)


def mirror_conj(part_re, part_im):
    lane_count = part_re.shape[-1]
    lane_index = jnp.arange(lane_count, dtype=jnp.int32)[None, :]
    flip_re = jnp.flip(part_re, axis=0)
    flip_im = jnp.flip(part_im, axis=0)
    mirror_re = jnp.where(lane_index < lane_count // 2, jnp.roll(flip_re, 1, axis=0), flip_re)
    mirror_im = -jnp.where(lane_index < lane_count // 2, jnp.roll(flip_im, 1, axis=0), flip_im)
    return (mirror_re, mirror_im)


def apply_filter(spec_re, spec_im, filt_re, filt_im, column):

    def plain_column(operand):
        return complex_product(spec_re, spec_im, filt_re, filt_im)

    def paired_column(operand):
        other_re, other_im = mirror_conj(filt_re, filt_im)
        plus_re = 0.25 * (filt_re + filt_im + other_re - other_im)
        plus_im = 0.25 * (filt_im - filt_re + other_im + other_re)
        minus_re = 0.25 * (filt_re - filt_im + other_re + other_im)
        minus_im = 0.25 * (filt_im + filt_re + other_im - other_re)
        mirror_re, mirror_im = mirror_conj(spec_re, spec_im)
        own_re, own_im = complex_product(spec_re, spec_im, plus_re, plus_im)
        side_re, side_im = complex_product(mirror_re, mirror_im, minus_re, minus_im)
        return (own_re + side_re, own_im + side_im)

    return lax.cond(column == 0, paired_column, plain_column, 0)


def body(values, long_filter, skip_gain):
    length_tok, lane_count = values.shape
    column_count = lax.axis_size("context")
    column = lax.axis_index("context")
    f_two = length_tok // F1
    seq_length = length_tok * column_count
    length = 2 * seq_length
    table_a = column_rows(column_count, 1.0, -1.0)
    table_b = column_rows(column_count, 2.0, -1.0)
    columns_all = jnp.arange(column_count, dtype=jnp.int32)
    own_column = column.reshape(1)
    shaped_values = values.reshape(1, F1, f_two, lane_count)
    shaped_filter = long_filter.reshape(1, F1, f_two, lane_count)
    twiddle_back = row_twiddle(f_two, length_tok, 1.0)
    a_count = F1 // column_count
    value_blocks, filter_blocks = (
        lax.all_to_all(shaped_values, "context", split_axis=1, concat_axis=0, tiled=True),
        lax.all_to_all(shaped_filter, "context", split_axis=1, concat_axis=0, tiled=True),
    )
    position_here = position_grid(column * a_count, a_count, f_two, f_two)
    twisted_values = first_columns(
        value_blocks, table_a, columns_all, position_here, column_count, length
    )
    twisted_filter = first_columns(
        filter_blocks, table_a, columns_all, position_here, column_count, length
    )
    twiddle_fwd = row_twiddle(f_two, length_tok, -1.0)
    spectrum = section_two(
        section_one(
            lax.all_to_all(twisted_values, "context", split_axis=0, concat_axis=2, tiled=True),
            twiddle_fwd,
        )
    )
    filter_spec = section_two(
        section_one(
            lax.all_to_all(twisted_filter, "context", split_axis=0, concat_axis=2, tiled=True),
            twiddle_fwd,
        )
    )
    out_re, out_im = apply_filter(
        spectrum[0, 0], spectrum[0, 1], filter_spec[0, 0], filter_spec[0, 1], column
    )
    filtered = jnp.stack([out_re, out_im], axis=0)[None].astype(jnp.bfloat16)
    back_half = back_two(filtered, twiddle_back)
    returned = back_one(
        back_half, own_column, position_grid(0, F1, f_two, f_two), column_count, length
    )
    gathered = lax.all_to_all(returned, "context", split_axis=2, concat_axis=0, tiled=True)
    conv_rows = last_rows(gathered, table_b, columns_all, length)
    convolved = lax.all_to_all(conv_rows, "context", split_axis=0, concat_axis=1, tiled=True)
    convolved = convolved.reshape(length_tok, lane_count)
    return (convolved.astype(jnp.float32) + skip_gain[None, :] * values.astype(jnp.float32)).astype(
        jnp.bfloat16
    )


def solution(mesh):
    return jax.shard_map(
        body,
        mesh=mesh,
        in_specs=(P("context", "tensor"), P("context", "tensor"), P("tensor")),
        out_specs=P("context", "tensor"),
        check_vma=False,
    )
```

profile of v0, /device:TPU:6, one launch (start us, length us, event | category | flops | bytes accessed | tf_op | source)
XLA Modules:
  0.0 164.9 jit_solution(2101805536101761779)
XLA Ops:
  0.0 13.7 %all-to-all-start = ((bf16[1,32,32,128]{3,2,0,1:T(8,128)(2,1)}), bf16[1,32,32,128]{3,2,0,1:T(8,128)(2,1)S(1)}, u32[]{:S(2)}, u32[]{:S(2)}) async-start(bf16[1,32,32,128]{3,2,0,1:T(8,128)(2,1)} %bitcast.314), calls=%async_computation | async-start | bytes 524288 | tf_op jit(solution)/shard_map/all_to_all | solution.py:172
  14.0 11.8 %all-to-all-done = bf16[1,32,32,128]{3,2,0,1:T(8,128)(2,1)S(1)} async-done(((bf16[1,32,32,128]{3,2,0,1:T(8,128)(2,1)}), bf16[1,32,32,128]{3,2,0,1:T(8,128)(2,1)S(1)}, u32[]{:S(2)}, u32[]{:S(2)}) %all-to-all-start) | async-done | bytes 262176 | tf_op jit(solution)/shard_map/all_to_all | solution.py:172
  25.7 4.6 %all-to-all-start.2 = ((bf16[1,32,32,128]{3,2,0,1:T(8,128)(2,1)}), bf16[1,32,32,128]{3,2,0,1:T(8,128)(2,1)S(1)}, u32[]{:S(2)}, u32[]{:S(2)}) async-start(bf16[1,32,32,128]{3,2,0,1:T(8,128)(2,1)} %bitcast.47), calls=%async_computation.2 | async-start | bytes 524288 | tf_op jit(solution)/shard_map/all_to_all | solution.py:173
  30.8 11.6 %all-to-all-done.2 = bf16[1,32,32,128]{3,2,0,1:T(8,128)(2,1)S(1)} async-done(((bf16[1,32,32,128]{3,2,0,1:T(8,128)(2,1)}), bf16[1,32,32,128]{3,2,0,1:T(8,128)(2,1)S(1)}, u32[]{:S(2)}, u32[]{:S(2)}) %all-to-all-start.2) | async-done | bytes 262176 | tf_op jit(solution)/shard_map/all_to_all | solution.py:173
  43.5 2.9 %subtract_convert_fusion.3 = (bf16[32,1,1,32,128]{4,0,3,1,2:T(8,128)(2,1)S(1)}, f32[32,1,1,32,128]{4,0,3,1,2:T(8,128)S(1)}, f32[32,1,1,32,128]{4,0,3,1,2:T(8,128...) fusion(s32[32,128]{1,0:T(8,128)S(1)} %iota_select_fusion, ...), kind=kLoop, calls=%fused_computation.101 | loop fusion | flops 3932160 | bytes 6832288 | tf_op jit(solution)/shard_map/convert.21
  46.5 2.6 %add_convert_fusion.5 = (bf16[32,1,1,32,128]{4,0,3,1,2:T(8,128)(2,1)S(1)}, bf16[32,1,1,32,128]{4,0,3,1,2:T(8,128)(2,1)S(1)}) fusion(f32[32,1,1,32,128]{4,0,3,1,2:T(8,128)S(1)} %get-tuple-element.46, f32[32,1,1,32,128]{4,0,3,1,2:T(8,128)S(1)} %get-tuple-element.45, s32[32,128]{1,0:T(8,128)S(1)} %iota_select_fusion, s32[32]{0:T(128)S(1)} %iota_add_fusion.1, ...), kind=kLoop, calls=%fused_computation.100 | loop fusion | flops 2883584 | bytes 2637952 | tf_op jit(solution)/shard_map/convert.22
  49.1 1.0 copy.75
  50.1 4.6 %all-to-all-start.1 = ((bf16[32,2,1,32,128]{4,3,1,2,0:T(8,128)(2,1)}), bf16[32,2,1,32,128]{4,3,1,2,0:T(8,128)(2,1)S(1)}, u32[]{:S(2)}, u32[]{:S(2)}) async-start(bf16[32,2,1,32,128]{4,3,1,2,0:T(8,128)(2,1)} %copy.75), calls=%async_computation.1 | async-start | bytes 1048576 | tf_op jit(solution)/shard_map/all_to_all | solution.py:185
  55.2 1.0 copy.89
  56.2 15.4 %all-to-all-done.1 = bf16[32,2,1,32,128]{4,3,1,2,0:T(8,128)(2,1)S(1)} async-done(((bf16[32,2,1,32,128]{4,3,1,2,0:T(8,128)(2,1)}), bf16[32,2,1,32,128]{4,3,1,2,0:T(8,128)(2,1)S(1)}, u32[]{:S(2)}, u32[]{:S(2)}) %all-to-all-start.1) | async-done | bytes 524320 | tf_op jit(solution)/shard_map/all_to_all | solution.py:185
  71.6 5.3 %all-to-all-start.3 = ((bf16[32,2,1,32,128]{4,3,1,2,0:T(8,128)(2,1)}), bf16[32,2,1,32,128]{4,3,1,2,0:T(8,128)(2,1)S(1)}, u32[]{:S(2)}, u32[]{:S(2)}) async-start(bf16[32,2,1,32,128]{4,3,1,2,0:T(8,128)(2,1)} %copy.89), calls=%async_computation.3 | async-start | bytes 1048576 | tf_op jit(solution)/shard_map/all_to_all | solution.py:191
  78.0 15.7 %all-to-all-done.3 = bf16[32,2,1,32,128]{4,3,1,2,0:T(8,128)(2,1)S(1)} async-done(((bf16[32,2,1,32,128]{4,3,1,2,0:T(8,128)(2,1)}), bf16[32,2,1,32,128]{4,3,1,2,0:T(8,128)(2,1)S(1)}, u32[]{:S(2)}, u32[]{:S(2)}) %all-to-all-start.3) | async-done | bytes 524320 | tf_op jit(solution)/shard_map/all_to_all | solution.py:191
  96.8 25.9 %conditional.1 = (bf16[1,32,32,128]{3,1,0,2:T(8,128)(2,1)S(1)}, bf16[1,32,32,128]{3,1,0,2:T(8,128)(2,1)S(1)}) conditional(s32[]{:T(128)} %convert_element_type.237, (f32[1024,128]{1,0:T(8,128)S(1)}, f32[1024,128]{1,0:T(8,128)S(1)}, f32[1024,128]{1,0:T(8,128)S(1)}, f32[1024,128]{1,0:T(8,128)S(1)}) %tuple.17, (f32[1024,128]{1,0:T(8,128)S(1)}, ...), branch_computations={%region_0.1_spmd, %region_1.2_spmd} | conditional | flops 6029440 | bytes 34075208 | solution.py:153
  98.2 3.7 %slice.95 = f32[1023,128]{1,0:T(8,128)S(1)} reverse(f32[1023,128]{1,0:T(8,128)} %slice.94), dimensions={0} | reverse | bytes 1047552 | tf_op jit(solution)/shard_map/cond/branch_1_fun/jit(_roll_static)/slice | solution.py:133
  102.0 2.6 %rev.10 = f32[1024,128]{1,0:T(8,128)} reverse(f32[1024,128]{1,0:T(8,128)S(1)} %get-tuple-element.29), dimensions={0} | reverse | bytes 1048576 | tf_op jit(solution)/shard_map/cond/branch_1_fun/jit(_flip)/rev | solution.py:131
  104.5 2.5 %rev.9 = f32[1024,128]{1,0:T(8,128)} reverse(f32[1024,128]{1,0:T(8,128)S(1)} %get-tuple-element.28), dimensions={0} | reverse | bytes 1048576 | tf_op jit(solution)/shard_map/cond/branch_1_fun/jit(_flip)/rev | solution.py:130
  107.1 2.3 %maximum_select_fusion = (f32[1024,128]{1,0:T(8,128)}, f32[1024,128]{1,0:T(8,128)}) fusion(f32[1024,128]{1,0:T(8,128)} %rev.9, f32[1023,128]{1,0:T(8,128)S(1)} %slice.92, f32[1,128]{1,0:T(1,128)S(1)} %slice.90, pred[128]{0:T(512)(128)(4,1)S(1)} %iota_compare_fusion, f32[1024,128]{1,0:T(8,128)} %rev.10, f32[1023,128]{1,0:T(8,128)S(1)} %slice.95, ...), kind=kLoop, calls=%fused_computation.2 | loop fusion | flops 655360 | bytes 3145856 | tf_op jit(solution)/shard_map/cond/branch_1_fun/jit(_where)/select_n | solution.py:132
  110.8 3.7 %slice.98 = f32[1023,128]{1,0:T(8,128)S(1)} reverse(f32[1023,128]{1,0:T(8,128)} %slice.97), dimensions={0} | reverse | bytes 1047552 | tf_op jit(solution)/shard_map/cond/branch_1_fun/jit(_roll_static)/slice | solution.py:132
  114.5 2.6 %rev.11 = f32[1024,128]{1,0:T(8,128)} reverse(f32[1024,128]{1,0:T(8,128)S(1)} %get-tuple-element.27), dimensions={0} | reverse | bytes 1048576 | tf_op jit(solution)/shard_map/cond/branch_1_fun/jit(_flip)/rev | solution.py:130
  117.1 2.5 %rev.12 = f32[1024,128]{1,0:T(8,128)} reverse(f32[1024,128]{1,0:T(8,128)S(1)} %get-tuple-element.30), dimensions={0} | reverse | bytes 1048576 | tf_op jit(solution)/shard_map/cond/branch_1_fun/jit(_flip)/rev | solution.py:131
  119.6 2.1 %add_convert_fusion.1 = (bf16[1024,128]{1,0:T(8,128)(2,1)S(1)}, f32[1024,128]{1,0:T(8,128)S(1)}, f32[1024,128]{1,0:T(8,128)S(1)}, f32[1024,128]{1,0:T(8,128)S(1)}, f32[1024,128]{1,0:T(8,128)S(1)}) fusion(f32[1024,128]{1,0:T(8,128)S(1)} %get-tuple-element.30, f32[1024,128]{1,0:T(8,128)S(1)} %get-tuple-element.27, f32[1024,128]{1,0:T(8,128)} %rev.11, ...), kind=kLoop, calls=%fused_computation.8 | loop fusion | flops 3670016 | bytes 7602304 | tf_op jit(solution)/shard_map/convert.16
  124.1 2.6 %subtract_convert_fusion.1 = (bf16[1,1,32,32,128]{4,2,1,3,0:T(8,128)(2,1)S(1)}, bf16[1,1,32,32,128]{4,2,1,3,0:T(8,128)(2,1)S(1)}) fusion(f32[1,2,32,32,128]{4,2,1,3,0:T(8,128)S(1)} %convolution_bitcast_fusion, s32[128]{0:T(128)S(1)} %broadcast_select_fusion, s32[32,32]{0,1:T(8,128)S(1)} %iota_add_fusion), kind=kLoop, calls=%fused_computation.97 | loop fusion | flops 2883584 | bytes 1577472 | tf_op jit(solution)/shard_map/convert.1
  127.1 18.9 %all_to_all.75 = bf16[1,2,32,32,128]{4,3,1,0,2:T(8,128)(2,1)S(1)} all-to-all(bf16[1,2,32,32,128]{4,3,1,0,2:T(8,128)(2,1)S(1)} %copy.103), channel_id=1, replica_groups=mesh['tensor'=16,'context'=32] {'context'}, dimensions={2} | all-to-all | bytes 1048576 | tf_op jit(solution)/shard_map/all_to_all | solution.py:203
  147.4 16.6 %all_to_all.76 = bf16[32,1,32,128]{3,2,1,0:T(8,128)(2,1)S(1)} all-to-all(bf16[32,1,32,128]{3,2,1,0:T(8,128)(2,1)S(1)} %copy.111), channel_id=1, replica_groups=mesh['tensor'=16,'context'=32] {'context'}, dimensions={0} | all-to-all | bytes 524288 | tf_op jit(solution)/shard_map/all_to_all | solution.py:205
  (78 shorter events, 13.9 us)
Async XLA Ops:
  0.0 25.7 %all-to-all-start = ((bf16[1,32,32,128]{3,2,0,1:T(8,128)(2,1)}), bf16[1,32,32,128]{3,2,0,1:T(8,128)(2,1)S(1)}, u32[]{:S(2)}, u32[]{:S(2)}) async-start(bf16[1,32,32,128]{3,2,0,1:T(8,128)(2,1)} %bitcast.314), calls=%async_computation | async-start | bytes 524288 | tf_op jit(solution)/shard_map/all_to_all | solution.py:172
  25.7 16.7 %all-to-all-start.2 = ((bf16[1,32,32,128]{3,2,0,1:T(8,128)(2,1)}), bf16[1,32,32,128]{3,2,0,1:T(8,128)(2,1)S(1)}, u32[]{:S(2)}, u32[]{:S(2)}) async-start(bf16[1,32,32,128]{3,2,0,1:T(8,128)(2,1)} %bitcast.47), calls=%async_computation.2 | async-start | bytes 524288 | tf_op jit(solution)/shard_map/all_to_all | solution.py:173
  50.1 21.5 %all-to-all-start.1 = ((bf16[32,2,1,32,128]{4,3,1,2,0:T(8,128)(2,1)}), bf16[32,2,1,32,128]{4,3,1,2,0:T(8,128)(2,1)S(1)}, u32[]{:S(2)}, u32[]{:S(2)}) async-start(bf16[32,2,1,32,128]{4,3,1,2,0:T(8,128)(2,1)} %copy.75), calls=%async_computation.1 | async-start | bytes 1048576 | tf_op jit(solution)/shard_map/all_to_all | solution.py:185
  71.6 22.1 %all-to-all-start.3 = ((bf16[32,2,1,32,128]{4,3,1,2,0:T(8,128)(2,1)}), bf16[32,2,1,32,128]{4,3,1,2,0:T(8,128)(2,1)S(1)}, u32[]{:S(2)}, u32[]{:S(2)}) async-start(bf16[32,2,1,32,128]{4,3,1,2,0:T(8,128)(2,1)} %copy.89), calls=%async_computation.3 | async-start | bytes 1048576 | tf_op jit(solution)/shard_map/all_to_all | solution.py:191
  119.6 2.1 %copy-start = (f32[1024,128]{1,0:T(8,128)S(1)}, f32[1024,128]{1,0:T(8,128)}, u32[]{:S(2)}) copy-start(f32[1024,128]{1,0:T(8,128)} %rev.11) | copy-start | bytes 1572868 | tf_op jit(solution)/shard_map/cond
  119.6 2.2 %copy-start.1 = (f32[1024,128]{1,0:T(8,128)S(1)}, f32[1024,128]{1,0:T(8,128)}, u32[]{:S(2)}) copy-start(f32[1024,128]{1,0:T(8,128)} %rev.12) | copy-start | bytes 1572868 | tf_op jit(solution)/shard_map/cond
  147.4 16.7 %copy-start.2 = (bf16[1024,128]{1,0:T(8,128)(2,1)S(1)}, bf16[1024,128]{1,0:T(8,128)(2,1)}, u32[]{:S(2)}) copy-start(bf16[1024,128]{1,0:T(8,128)(2,1)} %param.5) | copy-start | bytes 786436
  147.4 16.7 %copy-start.3 = (f32[128]{0:T(128)S(1)}, f32[128]{0:T(128)}, u32[]{:S(2)}) copy-start(f32[128]{0:T(128)} %param.7) | copy-start | bytes 1540
where the time goes:
time: 166 us; the launch traced here: 165 us
  waiting for transfers between devices  54.4 us (33%)
  blocking collectives  35.5 us (21%)
  starting transfers between devices  28.2 us (17%)
  local copies, waits for them, and re-layouts  26.2 us (16%)
  other arithmetic  16.6 us (10%)
  matrix products  3.19 us (2%)
    all_to_all x1, blocking collectives, body(): lax.all_to_all(returned, 'context', split_axis=2, concat_axis=0, tiled=True)  18.9 us
    all_to_all x1, blocking collectives, body(): lax.all_to_all(conv_rows, 'context', split_axis=0, concat_axis=1, tiled=T...  16.6 us
    all_to_all x1, waiting for transfers between devices, body(): lax.all_to_all(twisted_filter, 'context', split_axis=0, concat_axis=2, ti...  15.7 us
    all_to_all x1, waiting for transfers between devices, body(): lax.all_to_all(twisted_values, 'context', split_axis=0, concat_axis=2, ti...  15.4 us
    all_to_all x1, starting transfers between devices, body(): lax.all_to_all(shaped_values, 'context', split_axis=1, concat_axis=0, til...  13.7 us
    all_to_all x1, waiting for transfers between devices, body(): lax.all_to_all(shaped_values, 'context', split_axis=1, concat_axis=0, til...  11.8 us
    all_to_all x1, waiting for transfers between devices, body(): lax.all_to_all(shaped_filter, 'context', split_axis=1, concat_axis=0, til...  11.6 us
    another operation x10, other arithmetic  11.1 us
  transfers between devices with their start and end apart: 4, of which 4 were waited for; matrix products, arithmetic and copies ran while one was open for 2% of the time, Pallas kernels for 0%

commit v1 on v0

v1 whole, which is shorter than its diff:
```python
import math

import jax
import jax.numpy as jnp
import ml_dtypes
import numpy as np
from jax import lax
from jax.experimental import pallas as pl
from jax.experimental.pallas import tpu as pltpu
from jax.sharding import PartitionSpec as P

MESH = pl.DeviceIdType.MESH

N_DEV = 32
BLOCK = 1024
OWN = 4
HIGH, LOW = 8, 128
L1, L2 = 512, 128
N1 = L1 // 2
K1 = 272


def tables():
    length = L1 * L2
    k1 = np.arange(K1)
    n1 = np.arange(N1)
    n2 = np.arange(L2)
    kept = (k1 <= N1).astype(np.float64)[:, None]
    angle = 2 * math.pi * ((k1[:, None] * n1[None, :]) % L1) / L1
    first = np.concatenate([np.cos(angle) * kept, -np.sin(angle) * kept], axis=0)
    twist = 2 * math.pi * ((k1[:, None] * n2[None, :]) % length) / length
    angle = 2 * math.pi * ((n2[:, None] * n2[None, :]) % L2) / L2
    cosine, sine = np.cos(angle), np.sin(angle)
    second = np.block([[cosine, -sine], [sine, cosine]])
    back = np.block([[cosine, sine], [-sine, cosine]])
    k1 = np.arange(N1)
    angle = 2 * math.pi * ((n1[:, None] * k1[None, :]) % L1) / L1
    real = np.where(k1 == 0, 1.0, 2.0)[None, :] * np.cos(angle)
    imag = np.where(k1 == 0, (1.0 - 2.0 * (n1 % 2))[:, None], -2.0 * np.sin(angle))
    last = np.concatenate([real, imag], axis=1) / length
    half = ml_dtypes.bfloat16
    return (
        first.astype(half),
        np.cos(twist).astype(np.float32),
        np.sin(twist).astype(np.float32),
        second.astype(half),
        back.astype(half),
        last.astype(half),
    )


def dot(left, right):
    return jnp.dot(left, right, preferred_element_type=jnp.float32)


def kernel(
    values_ref,
    filter_ref,
    gain_ref,
    first_ref,
    cos_ref,
    sin_ref,
    second_ref,
    back_ref,
    last_ref,
    out_ref,
    wide,
    send,
    recv,
    line,
    spec,
    send_sem,
    recv_sem,
):
    me = lax.axis_index("context")
    barrier = pltpu.get_barrier_semaphore()

    def greet(k, carry):
        pl.semaphore_signal(
            barrier, inc=1, device_id={"context": lax.rem(me + k, N_DEV)}, device_id_type=MESH
        )
        return carry

    lax.fori_loop(1, N_DEV, greet, 0)

    def pack(source, slot):
        for high in range(HIGH):
            turned = source[high * LOW : (high + 1) * LOW, :].astype(jnp.float32).T
            for own in range(OWN):
                wide[own % 2, pl.ds((own // 2) * HIGH + high, N_DEV, stride=2 * HIGH), :] = turned[
                    own * N_DEV : (own + 1) * N_DEV, :
                ]
        for lower in range(2):
            send[slot, :, :, lower * LOW : (lower + 1) * LOW] = (
                wide[lower].astype(jnp.bfloat16).reshape(N_DEV, 2 * HIGH, LOW)
            )
        recv[slot, me] = send[slot, me]

    def copy_to(slot, device):
        return pltpu.make_async_remote_copy(
            src_ref=send.at[slot, device],
            dst_ref=recv.at[slot, me],
            send_sem=send_sem.at[slot],
            recv_sem=recv_sem.at[slot],
            device_id={"context": device},
            device_id_type=MESH,
        )

    def send_all(slot):
        def step(k, carry):
            copy_to(slot, lax.rem(me + k, N_DEV)).start()
            return carry

        lax.fori_loop(1, N_DEV, step, 0)

    def wait_all(buffer, slot, sem):
        blocks = buffer.at[slot, pl.ds(0, N_DEV - 1)]
        pltpu.make_async_copy(blocks, blocks, sem.at[slot]).wait()

    def spectrum(slot):
        rows = recv[slot].reshape(N_DEV * 2 * HIGH, 2 * LOW).astype(jnp.float32)
        rows = rows.reshape(N_DEV, 2, HIGH, 2 * LOW)
        for upper in range(2):
            part = rows[:, upper].reshape(N1, 2 * LOW).astype(jnp.bfloat16)
            summed = dot(first_ref[...], part)
            for lower in range(2):
                own = 2 * upper + lower
                real = summed[:K1, lower * LOW : (lower + 1) * LOW]
                imag = summed[K1:, lower * LOW : (lower + 1) * LOW]
                cosine, sine = cos_ref[...], sin_ref[...]
                line[own * K1 : (own + 1) * K1, :LOW] = (real * cosine + imag * sine).astype(
                    jnp.bfloat16
                )
                line[own * K1 : (own + 1) * K1, LOW:] = (imag * cosine - real * sine).astype(
                    jnp.bfloat16
                )
        return dot(line[...], second_ref[...])

    pack(filter_ref, 0)
    pl.semaphore_wait(barrier, N_DEV - 1)
    send_all(0)
    pack(values_ref, 1)
    send_all(1)

    wait_all(recv, 0, recv_sem)
    spec[...] = spectrum(0)
    wait_all(recv, 1, recv_sem)
    values_spec = spectrum(1)

    left_re, left_im = values_spec[:, :LOW], values_spec[:, LOW:]
    right_re, right_im = spec[:, :LOW], spec[:, LOW:]
    line[:, :LOW] = (left_re * right_re - left_im * right_im).astype(jnp.bfloat16)
    line[:, LOW:] = (left_re * right_im + left_im * right_re).astype(jnp.bfloat16)
    spec[...] = dot(line[...], back_ref[...])
    for upper in range(2):
        halves = []
        for lower in range(2):
            own = 2 * upper + lower
            real = spec[own * K1 : (own + 1) * K1, :LOW]
            imag = spec[own * K1 : (own + 1) * K1, LOW:]
            cosine, sine = cos_ref[...], sin_ref[...]
            turned_re = real * cosine - imag * sine
            turned_im = (imag * cosine + real * sine)[:N1]
            row = lax.broadcasted_iota(jnp.int32, (N1, LOW), 0)
            turned_im = jnp.where(row == 0, turned_re[N1 : N1 + 1], turned_im)
            halves.append(
                jnp.concatenate([turned_re[:N1], turned_im], axis=0).astype(jnp.bfloat16)
            )
        result = dot(last_ref[...], jnp.concatenate(halves, axis=1))
        result = result.reshape(N_DEV, HIGH, 2 * LOW)
        for device in range(N_DEV):
            start = device * 2 * HIGH + upper * HIGH
            for lower in range(2):
                wide[lower, start : start + HIGH, :] = result[
                    device, :, lower * LOW : (lower + 1) * LOW
                ]
    for lower in range(2):
        send[2, :, :, lower * LOW : (lower + 1) * LOW] = (
            wide[lower].astype(jnp.bfloat16).reshape(N_DEV, 2 * HIGH, LOW)
        )
    recv[2, me] = send[2, me]
    send_all(2)
    wait_all(recv, 2, recv_sem)
    for lower in range(2):
        wide[lower] = (
            recv[2, :, :, lower * LOW : (lower + 1) * LOW]
            .reshape(N_DEV * 2 * HIGH, LOW)
            .astype(jnp.float32)
        )
    for high in range(HIGH):
        turned = jnp.concatenate(
            [
                wide[own % 2, pl.ds((own // 2) * HIGH + high, N_DEV, stride=2 * HIGH), :]
                for own in range(OWN)
            ],
            axis=0,
        ).T
        direct = gain_ref[...] * values_ref[high * LOW : (high + 1) * LOW, :].astype(jnp.float32)
        out_ref[high * LOW : (high + 1) * LOW, :] = (turned + direct).astype(jnp.bfloat16)
    for slot in range(3):
        wait_all(send, slot, send_sem)


def body(values, long_filter, skip_gain):
    lanes = values.shape[1]
    vmem = pl.BlockSpec(memory_space=pltpu.VMEM)
    return pl.pallas_call(
        kernel,
        out_shape=jax.ShapeDtypeStruct(values.shape, jnp.bfloat16),
        in_specs=[vmem] * 9,
        out_specs=vmem,
        scratch_shapes=[
            pltpu.VMEM((2, N_DEV * 2 * HIGH, LOW), jnp.float32),
            pltpu.VMEM((3, N_DEV, 2 * HIGH, 2 * LOW), jnp.bfloat16),
            pltpu.VMEM((3, N_DEV, 2 * HIGH, 2 * LOW), jnp.bfloat16),
            pltpu.VMEM((OWN * K1, 2 * LOW), jnp.bfloat16),
            pltpu.VMEM((OWN * K1, 2 * LOW), jnp.float32),
            pltpu.SemaphoreType.DMA((3,)),
            pltpu.SemaphoreType.DMA((3,)),
        ],
        compiler_params=pltpu.CompilerParams(
            collective_id=0, has_side_effects=True, vmem_limit_bytes=40 * 2**20
        ),
    )(values, long_filter, skip_gain.reshape(1, lanes), *(jnp.asarray(t) for t in tables()))


def solution(mesh):
    return jax.shard_map(
        body,
        mesh=mesh,
        in_specs=(P("context", "tensor"), P("context", "tensor"), P("tensor")),
        out_specs=P("context", "tensor"),
        check_vma=False,
    )
```

time: 166 us -> 46.2 us (0.28)
  waiting for transfers between devices: 54.4 us -> 0 us
  Pallas kernels: 0 us -> 37.1 us
  blocking collectives: 35.5 us -> 0 us
  starting transfers between devices: 28.2 us -> 0 us
  local copies, waits for them, and re-layouts: 26.2 us -> 8.78 us
  other arithmetic: 16.6 us -> 0 us
  matrix products: 3.19 us -> 0 us
    all_to_all x4 -> x0, waiting for transfers between devices: 54.4 us -> none  [the longest x1 15.7 us: body(): lax.all_to_all(twisted_filter, 'context', split_axis=0, concat_axis=2, ti...]
    pallas_call x0 -> x1, Pallas kernels: none -> 37.1 us  [body(): pl.pallas_call(kernel, out_shape=jax.ShapeDtypeStruct(values.shape, jnp.b...]
    all_to_all x2 -> x0, blocking collectives: 35.5 us -> none  [the longest x1 18.9 us: body(): lax.all_to_all(returned, 'context', split_axis=2, concat_axis=0, tiled=True)]
    all_to_all x4 -> x0, starting transfers between devices: 28.2 us -> none  [the longest x1 13.7 us: body(): lax.all_to_all(shaped_values, 'context', split_axis=1, concat_axis=0, til...]
    another operation x21 -> x0, other arithmetic: 12.8 us -> none
    slice x12 -> x0, local copies, waits for them, and re-layouts: 10.3 us -> none  [the longest x6 5.13 us: mirror_conj(): jnp.roll(flip_re, 1, axis=0)]
    rev x4 -> x0, local copies, waits for them, and re-layouts: 10.2 us -> none  [the longest x2 5.11 us: mirror_conj(): flip_im = jnp.flip(part_im, axis=0)]
    unnamed x4 -> x19, local copies, waits for them, and re-layouts: 0.01 us -> 8.78 us
  transfers between devices with their start and end apart: 4 -> 0, of which waited for: 4 -> 0; matrix products, arithmetic and copies ran while one was open for 2% -> 0% of each run, Pallas kernels for 0% -> 0%
where the time goes in v1:
time: 46.2 us; the launch traced here: 45.9 us
  Pallas kernels  37.1 us (80%)
  local copies, waits for them, and re-layouts  8.78 us (19%)
    pallas_call x1, Pallas kernels, body(): pl.pallas_call(kernel, out_shape=jax.ShapeDtypeStruct(values.shape, jnp.b...  37.1 us
    unnamed x19, local copies, waits for them, and re-layouts  8.78 us

profile of v1, /device:TPU:6, one launch (start us, length us, event | category | flops | bytes accessed | tf_op | source)
XLA Modules:
  0.0 45.9 jit_solution(10690274228613746315)
XLA Ops:
  0.0 0.0 copy-start.8
  0.0 0.7 %copy-done.8 = f32[128]{0:T(128)S(1)} copy-done((f32[128]{0:T(128)S(1)}, f32[128]{0:T(128)}, u32[]{:S(2)}) %copy-start.8) | copy-done | bytes 536
  0.7 0.0 copy-start
  0.7 1.0 %copy-done = bf16[544,256]{1,0:T(8,128)(2,1)S(1)} copy-done((bf16[544,256]{1,0:T(8,128)(2,1)S(1)}, bf16[544,256]{1,0:T(8,128)(2,1)}, u32[]{:S(2)}) %copy-start) | copy-done | bytes 278552
  1.6 0.0 copy-start.1
  1.6 0.9 %copy-done.1 = bf16[1024,128]{1,0:T(8,128)(2,1)S(1)} copy-done((bf16[1024,128]{1,0:T(8,128)(2,1)S(1)}, bf16[1024,128]{1,0:T(8,128)(2,1)}, u32[]{:S(2)}) %copy-start.1) | copy-done | bytes 262168
  2.6 0.0 copy-start.2
  2.6 0.9 %copy-done.2 = bf16[1024,128]{1,0:T(8,128)(2,1)S(1)} copy-done((bf16[1024,128]{1,0:T(8,128)(2,1)S(1)}, bf16[1024,128]{1,0:T(8,128)(2,1)}, u32[]{:S(2)}) %copy-start.2) | copy-done | bytes 262168
  3.5 0.0 copy-start.3
  3.5 0.9 %copy-done.3 = bf16[256,512]{1,0:T(8,128)(2,1)S(1)} copy-done((bf16[256,512]{1,0:T(8,128)(2,1)S(1)}, bf16[256,512]{1,0:T(8,128)(2,1)}, u32[]{:S(2)}) %copy-start.3) | copy-done | bytes 262168
  4.5 0.0 copy-start.4
  4.5 0.9 %copy-done.4 = f32[272,128]{1,0:T(8,128)S(1)} copy-done((f32[272,128]{1,0:T(8,128)S(1)}, f32[272,128]{1,0:T(8,128)}, u32[]{:S(2)}) %copy-start.4) | copy-done | bytes 139288
  5.4 0.0 copy-start.5
  5.4 0.9 %copy-done.5 = f32[272,128]{1,0:T(8,128)S(1)} copy-done((f32[272,128]{1,0:T(8,128)S(1)}, f32[272,128]{1,0:T(8,128)}, u32[]{:S(2)}) %copy-start.5) | copy-done | bytes 139288
  6.3 0.0 copy-start.6
  6.3 0.9 %copy-done.6 = bf16[256,256]{1,0:T(8,128)(2,1)S(1)} copy-done((bf16[256,256]{1,0:T(8,128)(2,1)S(1)}, bf16[256,256]{1,0:T(8,128)(2,1)}, u32[]{:S(2)}) %copy-start.6) | copy-done | bytes 131096
  7.2 0.0 copy-start.7
  7.2 0.9 %copy-done.7 = bf16[256,256]{1,0:T(8,128)(2,1)S(1)} copy-done((bf16[256,256]{1,0:T(8,128)(2,1)S(1)}, bf16[256,256]{1,0:T(8,128)(2,1)}, u32[]{:S(2)}) %copy-start.7) | copy-done | bytes 131096
  8.1 37.1 %shard_map.91 = bf16[1024,128]{1,0:T(8,128)(2,1)S(1)} custom-call(bf16[1024,128]{1,0:T(8,128)(2,1)S(1)} %copy-done.1, bf16[1024,128]{1,0:T(8,128)(2,1)S(1)} %copy-done.2, f32[1,128]{1,0:T(1,128)S(1)} %bitcast.1, bf16[544,256]{1,0:T(8,128)(2,1)S(1)} %copy-done, f32[272,128]{1,0:T(8,128)S(1)} %copy-done.5, f32[272,128]{1,0:T(8,128)S(1)} %copy-done.4, ...), custom_call_target="tpu_custom_call" | custom-call | tf_op jit(solution)/shard_map/pallas_call | solution.py:207
  45.2 0.7 %copy.11 = bf16[1024,128]{1,0:T(8,128)(2,1)} copy(bf16[1024,128]{1,0:T(8,128)(2,1)S(1)} %shard_map.91) | data formatting | bytes 524288
Async XLA Ops:
  0.0 0.7 %copy-start.8 = (f32[128]{0:T(128)S(1)}, f32[128]{0:T(128)}, u32[]{:S(2)}) copy-start(f32[128]{0:T(128)} %param.11) | copy-start | bytes 1540
  0.7 1.0 %copy-start = (bf16[544,256]{1,0:T(8,128)(2,1)S(1)}, bf16[544,256]{1,0:T(8,128)(2,1)}, u32[]{:S(2)}) copy-start(bf16[544,256]{1,0:T(8,128)(2,1)} %constant.12.clone.first_ref) | copy-start | bytes 835588
  1.6 0.9 %copy-start.1 = (bf16[1024,128]{1,0:T(8,128)(2,1)S(1)}, bf16[1024,128]{1,0:T(8,128)(2,1)}, u32[]{:S(2)}) copy-start(bf16[1024,128]{1,0:T(8,128)(2,1)} %values_ref.1) | copy-start | bytes 786436
  2.6 0.9 %copy-start.2 = (bf16[1024,128]{1,0:T(8,128)(2,1)S(1)}, bf16[1024,128]{1,0:T(8,128)(2,1)}, u32[]{:S(2)}) copy-start(bf16[1024,128]{1,0:T(8,128)(2,1)} %filter_ref.1) | copy-start | bytes 786436
  3.5 0.9 %copy-start.3 = (bf16[256,512]{1,0:T(8,128)(2,1)S(1)}, bf16[256,512]{1,0:T(8,128)(2,1)}, u32[]{:S(2)}) copy-start(bf16[256,512]{1,0:T(8,128)(2,1)} %constant.17.clone.last_ref) | copy-start | bytes 786436
  4.5 0.9 %copy-start.4 = (f32[272,128]{1,0:T(8,128)S(1)}, f32[272,128]{1,0:T(8,128)}, u32[]{:S(2)}) copy-start(f32[272,128]{1,0:T(8,128)} %constant.14.clone.sin_ref) | copy-start | bytes 417796
  5.4 0.9 %copy-start.5 = (f32[272,128]{1,0:T(8,128)S(1)}, f32[272,128]{1,0:T(8,128)}, u32[]{:S(2)}) copy-start(f32[272,128]{1,0:T(8,128)} %constant.13.clone.cos_ref) | copy-start | bytes 417796
  6.3 0.9 %copy-start.6 = (bf16[256,256]{1,0:T(8,128)(2,1)S(1)}, bf16[256,256]{1,0:T(8,128)(2,1)}, u32[]{:S(2)}) copy-start(bf16[256,256]{1,0:T(8,128)(2,1)} %constant.16.clone.back_ref) | copy-start | bytes 393220
  7.2 0.9 %copy-start.7 = (bf16[256,256]{1,0:T(8,128)(2,1)S(1)}, bf16[256,256]{1,0:T(8,128)(2,1)}, u32[]{:S(2)}) copy-start(bf16[256,256]{1,0:T(8,128)(2,1)} %constant.15.clone.second_ref) | copy-start | bytes 393220

commit v2 on v1

v2 whole, which is shorter than its diff:
```python
import math

import jax
import jax.numpy as jnp
import ml_dtypes
import numpy as np
from jax import lax
from jax.experimental import pallas as pl
from jax.experimental.pallas import tpu as pltpu
from jax.sharding import PartitionSpec as P

MESH = pl.DeviceIdType.MESH

N_DEV = 32
BLOCK = 1024
OWN = 4
HIGH, LOW = 8, 128
L1, L2 = 512, 128
N1 = L1 // 2
K1 = 272


def tables():
    length = L1 * L2
    k1 = np.arange(K1)
    n1 = np.arange(N1)
    n2 = np.arange(L2)
    kept = (k1 <= N1).astype(np.float64)[:, None]
    angle = 2 * math.pi * ((k1[:, None] * n1[None, :]) % L1) / L1
    first = np.concatenate([np.cos(angle) * kept, -np.sin(angle) * kept], axis=0)
    twist = 2 * math.pi * ((k1[:, None] * n2[None, :]) % length) / length
    angle = 2 * math.pi * ((n2[:, None] * n2[None, :]) % L2) / L2
    cosine, sine = np.cos(angle), np.sin(angle)
    second = np.block([[cosine, -sine], [sine, cosine]])
    back = np.block([[cosine, sine], [-sine, cosine]])
    k1 = np.arange(N1)
    angle = 2 * math.pi * ((n1[:, None] * k1[None, :]) % L1) / L1
    real = np.where(k1 == 0, 1.0, 2.0)[None, :] * np.cos(angle)
    imag = np.where(k1 == 0, (1.0 - 2.0 * (n1 % 2))[:, None], -2.0 * np.sin(angle))
    last = np.concatenate([real, imag], axis=1) / length
    matrices = np.concatenate([first, second, back, last[:, :N1], last[:, N1:]], axis=0)
    twists = np.concatenate([np.cos(twist), np.sin(twist)], axis=0)
    return matrices.astype(ml_dtypes.bfloat16), twists.astype(np.float32)


def dot(left, right):
    return jnp.dot(left, right, preferred_element_type=jnp.float32)


def partner(me, k):
    turn, along_y = k // 4, lax.rem(k + 1, 4)
    along_z = 4 + (1 - 2 * lax.rem(turn, 2)) * ((turn + 1) // 2)
    y, z = me // 8, lax.rem(me, 8)
    return lax.rem(y + along_y, 4) * 8 + lax.rem(z + along_z, 8)


def kernel(
    filter_hbm,
    values_hbm,
    matrices_hbm,
    twists_hbm,
    out_ref,
    filter_ref,
    values_ref,
    matrices_ref,
    twists_ref,
    load_sem,
    wide,
    send_in,
    recv_in,
    send_out,
    recv_out,
    line,
    spec,
    send_sem,
    recv_sem,
):
    me = lax.axis_index("context")
    barrier = pltpu.get_barrier_semaphore()
    pairs = [
        (filter_hbm, filter_ref),
        (values_hbm, values_ref),
        (matrices_hbm, matrices_ref),
        (twists_hbm, twists_ref),
    ]
    loads = [
        pltpu.make_async_copy(source, target, load_sem.at[i])
        for i, (source, target) in enumerate(pairs)
    ]
    for load in loads:
        load.start()
    for k in range(N_DEV - 1):
        pl.semaphore_signal(
            barrier, inc=1, device_id={"context": partner(me, k)}, device_id_type=MESH
        )

    rows = [0, 2 * K1, 2 * K1 + 2 * LOW, 2 * K1 + 4 * LOW, 2 * K1 + 4 * LOW + N1]
    first, second, back, last_re, last_im = (
        matrices_ref.at[pl.ds(start, size)]
        for start, size in zip(rows, [2 * K1, 2 * LOW, 2 * LOW, N1, N1])
    )
    cos_ref, sin_ref = twists_ref.at[pl.ds(0, K1)], twists_ref.at[pl.ds(K1, K1)]

    def pack(source, lanes):
        for high in range(HIGH):
            turned = source[high * LOW : (high + 1) * LOW, :].astype(jnp.float32).T
            for own in range(OWN):
                wide[own // 2, pl.ds((own % 2) * HIGH + high, N_DEV, stride=2 * HIGH), :] = turned[
                    own * N_DEV : (own + 1) * N_DEV, :
                ]
        for half in range(2):
            send_in[half, :, :, lanes : lanes + LOW] = (
                wide[half].astype(jnp.bfloat16).reshape(N_DEV, 2 * HIGH, LOW)
            )

    def send_all(source, target, half, sem):
        def step(k, carry):
            device = partner(me, k)
            pltpu.make_async_remote_copy(
                src_ref=source.at[half, device],
                dst_ref=target.at[half, me],
                send_sem=send_sem.at[sem],
                recv_sem=recv_sem.at[sem],
                device_id={"context": device},
                device_id_type=MESH,
            ).start()
            return carry

        lax.fori_loop(0, N_DEV - 1, step, 0)
        target[half, me] = source[half, me]

    def wait_all(buffer, half, sem):
        blocks = buffer.at[half, pl.ds(0, N_DEV - 1)]
        pltpu.make_async_copy(blocks, blocks, sem).wait()

    def convolve(half):
        rows = recv_in[half].reshape(N_DEV * 2 * HIGH, 2 * LOW).astype(jnp.float32)
        rows = rows.reshape(N_DEV, 2, HIGH, 2 * LOW)
        cosine, sine = cos_ref[...], sin_ref[...]
        for own in range(2):
            part = rows[:, own].reshape(N1, 2 * LOW).astype(jnp.bfloat16)
            summed = dot(first[...], part)
            for array in range(2):
                start = (2 * array + own) * K1
                real = summed[:K1, array * LOW : (array + 1) * LOW]
                imag = summed[K1:, array * LOW : (array + 1) * LOW]
                line[start : start + K1, :LOW] = (real * cosine + imag * sine).astype(jnp.bfloat16)
                line[start : start + K1, LOW:] = (imag * cosine - real * sine).astype(jnp.bfloat16)
        spec[...] = dot(line[...], second[...])
        left_re, left_im = spec[: 2 * K1, :LOW], spec[: 2 * K1, LOW:]
        right_re, right_im = spec[2 * K1 :, :LOW], spec[2 * K1 :, LOW:]
        line[: 2 * K1, :LOW] = (left_re * right_re - left_im * right_im).astype(jnp.bfloat16)
        line[: 2 * K1, LOW:] = (left_re * right_im + left_im * right_re).astype(jnp.bfloat16)
        spec[: 2 * K1, :] = dot(line[: 2 * K1, :], back[...])
        columns_re, columns_im = [], []
        for own in range(2):
            real = spec[own * K1 : (own + 1) * K1, :LOW]
            imag = spec[own * K1 : (own + 1) * K1, LOW:]
            turned_re = real * cosine - imag * sine
            turned_im = (imag * cosine + real * sine)[:N1]
            row = lax.broadcasted_iota(jnp.int32, (N1, LOW), 0)
            turned_im = jnp.where(row == 0, turned_re[N1 : N1 + 1], turned_im)
            columns_re.append(turned_re[:N1].astype(jnp.bfloat16))
            columns_im.append(turned_im.astype(jnp.bfloat16))
        result = dot(last_re[...], jnp.concatenate(columns_re, axis=1))
        result += dot(last_im[...], jnp.concatenate(columns_im, axis=1))
        result = jnp.stack(
            [result[:, own * LOW : (own + 1) * LOW].reshape(N_DEV, HIGH, LOW) for own in range(2)],
            axis=1,
        )
        send_out[half] = result.reshape(N_DEV, 2 * HIGH, LOW).astype(jnp.bfloat16)

    loads[0].wait()
    pack(filter_ref, LOW)
    loads[1].wait()
    pack(values_ref, 0)
    pl.semaphore_wait(barrier, N_DEV - 1)
    for half in range(2):
        send_all(send_in, recv_in, half, half)
    for load in loads[2:]:
        load.wait()
    for half in range(2):
        wait_all(recv_in, half, recv_sem.at[half])
        convolve(half)
        send_all(send_out, recv_out, half, 2 + half)
    for half in range(2):
        wait_all(recv_out, half, recv_sem.at[2 + half])
        wide[half] = recv_out[half].reshape(N_DEV * 2 * HIGH, LOW).astype(jnp.float32)
    for high in range(HIGH):
        turned = jnp.concatenate(
            [
                wide[own // 2, pl.ds((own % 2) * HIGH + high, N_DEV, stride=2 * HIGH), :]
                for own in range(OWN)
            ],
            axis=0,
        ).T
        out_ref[high * LOW : (high + 1) * LOW, :] = turned.astype(jnp.bfloat16)
    for half in range(2):
        wait_all(send_in, half, send_sem.at[half])
        wait_all(send_out, half, send_sem.at[2 + half])


def body(values, long_filter, skip_gain):
    operands = (long_filter, values, *(jnp.asarray(t) for t in tables()))
    convolved = pl.pallas_call(
        kernel,
        out_shape=jax.ShapeDtypeStruct(values.shape, jnp.bfloat16),
        in_specs=[pl.BlockSpec(memory_space=pltpu.HBM)] * len(operands),
        out_specs=pl.BlockSpec(memory_space=pltpu.VMEM),
        scratch_shapes=[
            *(pltpu.VMEM(x.shape, x.dtype) for x in operands),
            pltpu.SemaphoreType.DMA((len(operands),)),
            pltpu.VMEM((2, N_DEV * 2 * HIGH, LOW), jnp.float32),
            pltpu.VMEM((2, N_DEV, 2 * HIGH, 2 * LOW), jnp.bfloat16),
            pltpu.VMEM((2, N_DEV, 2 * HIGH, 2 * LOW), jnp.bfloat16),
            pltpu.VMEM((2, N_DEV, 2 * HIGH, LOW), jnp.bfloat16),
            pltpu.VMEM((2, N_DEV, 2 * HIGH, LOW), jnp.bfloat16),
            pltpu.VMEM((OWN * K1, 2 * LOW), jnp.bfloat16),
            pltpu.VMEM((OWN * K1, 2 * LOW), jnp.float32),
            pltpu.SemaphoreType.DMA((4,)),
            pltpu.SemaphoreType.DMA((4,)),
        ],
        compiler_params=pltpu.CompilerParams(
            collective_id=0, has_side_effects=True, vmem_limit_bytes=107 * 2**19
        ),
    )(*operands)
    direct = skip_gain[None, :] * values.astype(jnp.float32)
    return (convolved.astype(jnp.float32) + direct).astype(jnp.bfloat16)


def solution(mesh):
    return jax.shard_map(
        body,
        mesh=mesh,
        in_specs=(P("context", "tensor"), P("context", "tensor"), P("tensor")),
        out_specs=P("context", "tensor"),
        check_vma=False,
    )
```

time: 46.2 us -> 36.6 us (0.79)
  local copies, waits for them, and re-layouts: 8.78 us -> 0.01 us
  Pallas kernels: 37.1 us -> 35.5 us
  other arithmetic: 0 us -> 0.79 us
    unnamed x19 -> x4, local copies, waits for them, and re-layouts: 8.78 us -> 0.01 us
    pallas_call x1, Pallas kernels: 37.1 us -> 35.5 us  [body(): pl.pallas_call(kernel, out_shape=jax.ShapeDtypeStruct(values.shape, jnp.b...]
    convert_element_type x0 -> x1, other arithmetic: none -> 0.79 us  [body(): return (convolved.astype(jnp.float32) + direct).astype(jnp.bfloat16)]
where the time goes in v2:
time: 36.6 us; the launch traced here: 36.4 us
  Pallas kernels  35.5 us (97%)
  other arithmetic  0.79 us (2%)
    pallas_call x1, Pallas kernels, body(): pl.pallas_call(kernel, out_shape=jax.ShapeDtypeStruct(values.shape, jnp.b...  35.5 us
    convert_element_type x1, other arithmetic, body(): return (convolved.astype(jnp.float32) + direct).astype(jnp.bfloat16)  0.79 us

profile of v2, /device:TPU:6, one launch (start us, length us, event | category | flops | bytes accessed | tf_op | source)
XLA Modules:
  0.0 36.4 jit_solution(8831511749689518652)
XLA Ops:
  0.0 0.0 copy-start
  0.0 0.0 copy-start.1
  0.0 35.5 %shard_map.55 = bf16[1024,128]{1,0:T(8,128)(2,1)S(1)} custom-call(bf16[1024,128]{1,0:T(8,128)(2,1)} %filter_hbm.1, bf16[1024,128]{1,0:T(8,128)(2,1)} %values_hbm.1, bf16[1568,256]{1,0:T(8,128)(2,1)} %constant.4.clone.matrices_hbm, f32[544,128]{1,0:T(8,128)} %constant.5.clone.twists_hbm), custom_call_target="tpu_custom_call" | custom-call | tf_op jit(solution)/shard_map/pallas_call | solution.py:205
  35.5 0.0 copy-done
  35.6 0.0 copy-done.1
  35.6 0.8 %add_convert_fusion = bf16[1024,128]{1,0:T(8,128)(2,1)} fusion(bf16[1024,128]{1,0:T(8,128)(2,1)S(1)} %copy-done, bf16[1024,128]{1,0:T(8,128)(2,1)S(1)} %shard_map.55, f32[128]{0:T(128)S(1)} %copy-done.1), kind=kLoop, calls=%fused_computation | loop fusion | flops 655360 | bytes 786944 | tf_op jit(solution)/shard_map/convert_element_type | solution.py:228
Async XLA Ops:
  0.0 35.5 %copy-start = (bf16[1024,128]{1,0:T(8,128)(2,1)S(1)}, bf16[1024,128]{1,0:T(8,128)(2,1)}, u32[]{:S(2)}) copy-start(bf16[1024,128]{1,0:T(8,128)(2,1)} %values_hbm.1) | copy-start | bytes 786436
  0.0 35.6 %copy-start.1 = (f32[128]{0:T(128)S(1)}, f32[128]{0:T(128)}, u32[]{:S(2)}) copy-start(f32[128]{0:T(128)} %param.7) | copy-start | bytes 1540

commit v3 on v2

--- a/solution.py
+++ b/solution.py
@@ -70,8 +70,6 @@
     recv_in,
     send_out,
     recv_out,
-    line,
-    spec,
     send_sem,
     recv_sem,
 ):
@@ -114,7 +112,7 @@
             )
 
     def send_all(source, target, half, sem):
-        def step(k, carry):
+        for k in range(N_DEV - 1):
             device = partner(me, k)
             pltpu.make_async_remote_copy(
                 src_ref=source.at[half, device],
@@ -124,10 +122,26 @@
                 device_id={"context": device},
                 device_id_type=MESH,
             ).start()
-            return carry
-
-        lax.fori_loop(0, N_DEV - 1, step, 0)
         target[half, me] = source[half, me]
+
+    def send_back(half):
+        y, z = me // 8, lax.rem(me, 8)
+        for k in range(N_DEV):
+            to_z, turn = k // 4, (k + 1) % 4
+            device = lax.rem(y + turn, 4) * 8 + to_z
+            copy = pltpu.make_async_remote_copy(
+                src_ref=send_out.at[half, device],
+                dst_ref=recv_out.at[half, me],
+                send_sem=send_sem.at[2 + half],
+                recv_sem=recv_sem.at[2 + half],
+                device_id={"context": device},
+                device_id_type=MESH,
+            )
+            if turn:
+                copy.start()
+            else:
+                pl.when(z != to_z)(copy.start)
+        recv_out[half, me] = send_out[half, me]
 
     def wait_all(buffer, half, sem):
         blocks = buffer.at[half, pl.ds(0, N_DEV - 1)]
@@ -137,33 +151,49 @@
         rows = recv_in[half].reshape(N_DEV * 2 * HIGH, 2 * LOW).astype(jnp.float32)
         rows = rows.reshape(N_DEV, 2, HIGH, 2 * LOW)
         cosine, sine = cos_ref[...], sin_ref[...]
+        row = lax.broadcasted_iota(jnp.int32, (N1, LOW), 0)
+        columns_re, columns_im = [], []
+        lines = []
         for own in range(2):
             part = rows[:, own].reshape(N1, 2 * LOW).astype(jnp.bfloat16)
-            summed = dot(first[...], part)
+            summed_re, summed_im = dot(first[:K1, :], part), dot(first[K1:, :], part)
             for array in range(2):
-                start = (2 * array + own) * K1
-                real = summed[:K1, array * LOW : (array + 1) * LOW]
-                imag = summed[K1:, array * LOW : (array + 1) * LOW]
-                line[start : start + K1, :LOW] = (real * cosine + imag * sine).astype(jnp.bfloat16)
-                line[start : start + K1, LOW:] = (imag * cosine - real * sine).astype(jnp.bfloat16)
-        spec[...] = dot(line[...], second[...])
-        left_re, left_im = spec[: 2 * K1, :LOW], spec[: 2 * K1, LOW:]
-        right_re, right_im = spec[2 * K1 :, :LOW], spec[2 * K1 :, LOW:]
-        line[: 2 * K1, :LOW] = (left_re * right_re - left_im * right_im).astype(jnp.bfloat16)
-        line[: 2 * K1, LOW:] = (left_re * right_im + left_im * right_re).astype(jnp.bfloat16)
-        spec[: 2 * K1, :] = dot(line[: 2 * K1, :], back[...])
-        columns_re, columns_im = [], []
+                real = summed_re[:, array * LOW : (array + 1) * LOW]
+                imag = summed_im[:, array * LOW : (array + 1) * LOW]
+                lines.append(jnp.concatenate(
+                    [
+                        (real * cosine + imag * sine).astype(jnp.bfloat16),
+                        (imag * cosine - real * sine).astype(jnp.bfloat16),
+                    ],
+                    axis=1,
+                ))
+        spectra = [dot(l, second[...]) for l in lines]
+        products = []
         for own in range(2):
-            real = spec[own * K1 : (own + 1) * K1, :LOW]
-            imag = spec[own * K1 : (own + 1) * K1, LOW:]
+            left_re, left_im = spectra[2*own][:, :LOW], spectra[2*own][:, LOW:]
+            right_re, right_im = spectra[2*own+1][:, :LOW], spectra[2*own+1][:, LOW:]
+            products.append(jnp.concatenate(
+                [
+                    (left_re * right_re - left_im * right_im).astype(jnp.bfloat16),
+                    (left_re * right_im + left_im * right_re).astype(jnp.bfloat16),
+                ],
+                axis=1,
+            ))
+        turneds = [dot(p, back[...]) for p in products]
+        for own in range(2):
+            turned = turneds[own]
+            real, imag = turned[:, :LOW], turned[:, LOW:]
             turned_re = real * cosine - imag * sine
             turned_im = (imag * cosine + real * sine)[:N1]
-            row = lax.broadcasted_iota(jnp.int32, (N1, LOW), 0)
             turned_im = jnp.where(row == 0, turned_re[N1 : N1 + 1], turned_im)
             columns_re.append(turned_re[:N1].astype(jnp.bfloat16))
             columns_im.append(turned_im.astype(jnp.bfloat16))
-        result = dot(last_re[...], jnp.concatenate(columns_re, axis=1))
-        result += dot(last_im[...], jnp.concatenate(columns_im, axis=1))
+        result = dot(
+            jnp.concatenate([last_re[...], last_im[...]], axis=1),
+            jnp.concatenate(
+                [jnp.concatenate(columns_re, axis=1), jnp.concatenate(columns_im, axis=1)], axis=0
+            ),
+        )
         result = jnp.stack(
             [result[:, own * LOW : (own + 1) * LOW].reshape(N_DEV, HIGH, LOW) for own in range(2)],
             axis=1,
@@ -182,7 +212,7 @@
     for half in range(2):
         wait_all(recv_in, half, recv_sem.at[half])
         convolve(half)
-        send_all(send_out, recv_out, half, 2 + half)
+        send_back(half)
     for half in range(2):
         wait_all(recv_out, half, recv_sem.at[2 + half])
         wide[half] = recv_out[half].reshape(N_DEV * 2 * HIGH, LOW).astype(jnp.float32)
@@ -215,8 +245,6 @@
             pltpu.VMEM((2, N_DEV, 2 * HIGH, 2 * LOW), jnp.bfloat16),
             pltpu.VMEM((2, N_DEV, 2 * HIGH, LOW), jnp.bfloat16),
             pltpu.VMEM((2, N_DEV, 2 * HIGH, LOW), jnp.bfloat16),
-            pltpu.VMEM((OWN * K1, 2 * LOW), jnp.bfloat16),
-            pltpu.VMEM((OWN * K1, 2 * LOW), jnp.float32),
             pltpu.SemaphoreType.DMA((4,)),
             pltpu.SemaphoreType.DMA((4,)),
         ],

time: 36.6 us -> 36.4 us (level)
  no operation moved by 1% of the time
where the time goes in v3:
time: 36.4 us; the launch traced here: 36.3 us
  Pallas kernels  35.4 us (97%)
  other arithmetic  0.79 us (2%)
    pallas_call x1, Pallas kernels, body(): pl.pallas_call(kernel, out_shape=jax.ShapeDtypeStruct(values.shape, jnp.b...  35.4 us
    convert_element_type x1, other arithmetic, body(): return (convolved.astype(jnp.float32) + direct).astype(jnp.bfloat16)  0.79 us

profile of v3, /device:TPU:6, one launch (start us, length us, event | category | flops | bytes accessed | tf_op | source)
XLA Modules:
  0.0 36.3 jit_solution(6871506233194318780)
XLA Ops:
  0.0 0.0 copy-start
  0.0 0.0 copy-start.1
  0.0 35.4 %shard_map.55 = bf16[1024,128]{1,0:T(8,128)(2,1)S(1)} custom-call(bf16[1024,128]{1,0:T(8,128)(2,1)} %filter_hbm.1, bf16[1024,128]{1,0:T(8,128)(2,1)} %values_hbm.1, bf16[1568,256]{1,0:T(8,128)(2,1)} %constant.4.clone.matrices_hbm, f32[544,128]{1,0:T(8,128)} %constant.5.clone.twists_hbm), custom_call_target="tpu_custom_call" | custom-call | tf_op jit(solution)/shard_map/pallas_call | solution.py:235
  35.4 0.0 copy-done
  35.5 0.0 copy-done.1
  35.5 0.8 %add_convert_fusion = bf16[1024,128]{1,0:T(8,128)(2,1)} fusion(bf16[1024,128]{1,0:T(8,128)(2,1)S(1)} %copy-done, bf16[1024,128]{1,0:T(8,128)(2,1)S(1)} %shard_map.55, f32[128]{0:T(128)S(1)} %copy-done.1), kind=kLoop, calls=%fused_computation | loop fusion | flops 655360 | bytes 786944 | tf_op jit(solution)/shard_map/convert_element_type | solution.py:256
Async XLA Ops:
  0.0 35.4 %copy-start = (bf16[1024,128]{1,0:T(8,128)(2,1)S(1)}, bf16[1024,128]{1,0:T(8,128)(2,1)}, u32[]{:S(2)}) copy-start(bf16[1024,128]{1,0:T(8,128)(2,1)} %values_hbm.1) | copy-start | bytes 786436
  0.0 35.5 %copy-start.1 = (f32[128]{0:T(128)S(1)}, f32[128]{0:T(128)}, u32[]{:S(2)}) copy-start(f32[128]{0:T(128)} %param.7) | copy-start | bytes 1540

commit v4 on v3

--- a/solution.py
+++ b/solution.py
@@ -17,6 +17,8 @@
 HIGH, LOW = 8, 128
 L1, L2 = 512, 128
 N1 = L1 // 2
+FAR_FIRST = [(y, z) for z in (4, 3, 5, 2, 6, 1, 7, 0) for y in (1, 2, 3, 0) if (y, z) != (0, 0)]
+MIXED = [(y, z) for y in (2, 1, 3, 0) for z in (3, 5, 2, 6, 4, 1, 7, 0) if (y, z) != (0, 0)]
 K1 = 272
 
 
@@ -47,13 +49,6 @@
     return jnp.dot(left, right, preferred_element_type=jnp.float32)
 
 
-def partner(me, k):
-    turn, along_y = k // 4, lax.rem(k + 1, 4)
-    along_z = 4 + (1 - 2 * lax.rem(turn, 2)) * ((turn + 1) // 2)
-    y, z = me // 8, lax.rem(me, 8)
-    return lax.rem(y + along_y, 4) * 8 + lax.rem(z + along_z, 8)
-
-
 def kernel(
     filter_hbm,
     values_hbm,
@@ -74,7 +69,12 @@
     recv_sem,
 ):
     me = lax.axis_index("context")
+    my_y, my_z = me // 8, lax.rem(me, 8)
     barrier = pltpu.get_barrier_semaphore()
+
+    def partner(steps):
+        return lax.rem(my_y + steps[0], 4) * 8 + lax.rem(my_z + steps[1], 8)
+
     pairs = [
         (filter_hbm, filter_ref),
         (values_hbm, values_ref),
@@ -85,12 +85,13 @@
         pltpu.make_async_copy(source, target, load_sem.at[i])
         for i, (source, target) in enumerate(pairs)
     ]
-    for load in loads:
+    loads[0].start()
+    for steps in FAR_FIRST:
+        pl.semaphore_signal(
+            barrier, inc=1, device_id={"context": partner(steps)}, device_id_type=MESH
+        )
+    for load in loads[1:]:
         load.start()
-    for k in range(N_DEV - 1):
-        pl.semaphore_signal(
-            barrier, inc=1, device_id={"context": partner(me, k)}, device_id_type=MESH
-        )
 
     rows = [0, 2 * K1, 2 * K1 + 2 * LOW, 2 * K1 + 4 * LOW, 2 * K1 + 4 * LOW + N1]
     first, second, back, last_re, last_im = (
@@ -111,36 +112,30 @@
                 wide[half].astype(jnp.bfloat16).reshape(N_DEV, 2 * HIGH, LOW)
             )
 
-    def send_all(source, target, half, sem):
-        for k in range(N_DEV - 1):
-            device = partner(me, k)
-            pltpu.make_async_remote_copy(
-                src_ref=source.at[half, device],
-                dst_ref=target.at[half, me],
-                send_sem=send_sem.at[sem],
-                recv_sem=recv_sem.at[sem],
-                device_id={"context": device},
-                device_id_type=MESH,
-            ).start()
-        target[half, me] = source[half, me]
+    def copy_to(source, target, half, sem, device):
+        return pltpu.make_async_remote_copy(
+            src_ref=source.at[half, device],
+            dst_ref=target.at[half, me],
+            send_sem=send_sem.at[sem],
+            recv_sem=recv_sem.at[sem],
+            device_id={"context": device},
+            device_id_type=MESH,
+        )
+
+    def send_blocks(half):
+        for steps in MIXED:
+            copy_to(send_in, recv_in, half, half, partner(steps)).start()
+        recv_in[half, me] = send_in[half, me]
 
     def send_back(half):
-        y, z = me // 8, lax.rem(me, 8)
         for k in range(N_DEV):
             to_z, turn = k // 4, (k + 1) % 4
-            device = lax.rem(y + turn, 4) * 8 + to_z
-            copy = pltpu.make_async_remote_copy(
-                src_ref=send_out.at[half, device],
-                dst_ref=recv_out.at[half, me],
-                send_sem=send_sem.at[2 + half],
-                recv_sem=recv_sem.at[2 + half],
-                device_id={"context": device},
-                device_id_type=MESH,
-            )
+            device = lax.rem(my_y + turn, 4) * 8 + to_z
+            copy = copy_to(send_out, recv_out, half, 2 + half, device)
             if turn:
                 copy.start()
             else:
-                pl.when(z != to_z)(copy.start)
+                pl.when(my_z != to_z)(copy.start)
         recv_out[half, me] = send_out[half, me]
 
     def wait_all(buffer, half, sem):
@@ -206,7 +201,7 @@
     pack(values_ref, 0)
     pl.semaphore_wait(barrier, N_DEV - 1)
     for half in range(2):
-        send_all(send_in, recv_in, half, half)
+        send_blocks(half)
     for load in loads[2:]:
         load.wait()
     for half in range(2):

time: 36.4 us -> 35.9 us (0.986)
  Pallas kernels: 35.4 us -> 35 us
    pallas_call x1, Pallas kernels: 35.4 us -> 35 us  [body(): pl.pallas_call(kernel, out_shape=jax.ShapeDtypeStruct(values.shape, jnp.b...]
where the time goes in v4:
time: 35.9 us; the launch traced here: 35.8 us
  Pallas kernels  35 us (97%)
  other arithmetic  0.79 us (2%)
    pallas_call x1, Pallas kernels, body(): pl.pallas_call(kernel, out_shape=jax.ShapeDtypeStruct(values.shape, jnp.b...  35 us
    convert_element_type x1, other arithmetic, body(): return (convolved.astype(jnp.float32) + direct).astype(jnp.bfloat16)  0.79 us

profile of v4, /device:TPU:6, one launch (start us, length us, event | category | flops | bytes accessed | tf_op | source)
XLA Modules:
  0.0 35.8 jit_solution(17783065696955253496)
XLA Ops:
  0.0 0.0 copy-start
  0.0 0.0 copy-start.1
  0.0 35.0 %shard_map.55 = bf16[1024,128]{1,0:T(8,128)(2,1)S(1)} custom-call(bf16[1024,128]{1,0:T(8,128)(2,1)} %filter_hbm.1, bf16[1024,128]{1,0:T(8,128)(2,1)} %values_hbm.1, bf16[1568,256]{1,0:T(8,128)(2,1)} %constant.4.clone.matrices_hbm, f32[544,128]{1,0:T(8,128)} %constant.5.clone.twists_hbm), custom_call_target="tpu_custom_call" | custom-call | tf_op jit(solution)/shard_map/pallas_call | solution.py:230
  35.0 0.0 copy-done
  35.0 0.0 copy-done.1
  35.0 0.8 %add_convert_fusion = bf16[1024,128]{1,0:T(8,128)(2,1)} fusion(bf16[1024,128]{1,0:T(8,128)(2,1)S(1)} %copy-done, bf16[1024,128]{1,0:T(8,128)(2,1)S(1)} %shard_map.55, f32[128]{0:T(128)S(1)} %copy-done.1), kind=kLoop, calls=%fused_computation | loop fusion | flops 655360 | bytes 786944 | tf_op jit(solution)/shard_map/convert_element_type | solution.py:251
Async XLA Ops:
  0.0 35.0 %copy-start = (bf16[1024,128]{1,0:T(8,128)(2,1)S(1)}, bf16[1024,128]{1,0:T(8,128)(2,1)}, u32[]{:S(2)}) copy-start(bf16[1024,128]{1,0:T(8,128)(2,1)} %values_hbm.1) | copy-start | bytes 786436
  0.0 35.0 %copy-start.1 = (f32[128]{0:T(128)S(1)}, f32[128]{0:T(128)}, u32[]{:S(2)}) copy-start(f32[128]{0:T(128)} %param.7) | copy-start | bytes 1540

commit v5 on v4

--- a/solution.py
+++ b/solution.py
@@ -90,6 +90,11 @@
         pl.semaphore_signal(
             barrier, inc=1, device_id={"context": partner(steps)}, device_id_type=MESH
         )
+    lane = lax.axis_index("tensor")
+    sibling = lane + 1 - 2 * lax.rem(lane, 2)
+    pl.semaphore_signal(
+        barrier, inc=1, device_id={"tensor": sibling, "context": me}, device_id_type=MESH
+    )
     for load in loads[1:]:
         load.start()
 
@@ -199,7 +204,7 @@
     pack(filter_ref, LOW)
     loads[1].wait()
     pack(values_ref, 0)
-    pl.semaphore_wait(barrier, N_DEV - 1)
+    pl.semaphore_wait(barrier, N_DEV)
     for half in range(2):
         send_blocks(half)
     for load in loads[2:]:
@@ -210,8 +215,18 @@
         send_back(half)
     for half in range(2):
         wait_all(recv_out, half, recv_sem.at[2 + half])
-        wide[half] = recv_out[half].reshape(N_DEV * 2 * HIGH, LOW).astype(jnp.float32)
+        out_ref[half] = recv_out[half]
+    for half in range(2):
+        wait_all(send_in, half, send_sem.at[half])
+        wait_all(send_out, half, send_sem.at[2 + half])
+
+
+def finish(blocks_ref, values_ref, gain_ref, out_hbm, wide, staged, sem):
+    for half in range(2):
+        wide[half] = blocks_ref[half].reshape(N_DEV * 2 * HIGH, LOW).astype(jnp.float32)
+    copies = []
     for high in range(HIGH):
+        rows = pl.ds(high * LOW, LOW)
         turned = jnp.concatenate(
             [
                 wide[own // 2, pl.ds((own % 2) * HIGH + high, N_DEV, stride=2 * HIGH), :]
@@ -219,17 +234,20 @@
             ],
             axis=0,
         ).T
-        out_ref[high * LOW : (high + 1) * LOW, :] = turned.astype(jnp.bfloat16)
-    for half in range(2):
-        wait_all(send_in, half, send_sem.at[half])
-        wait_all(send_out, half, send_sem.at[2 + half])
+        direct = gain_ref[...] * values_ref[rows, :].astype(jnp.float32)
+        staged[rows, :] = (turned + direct).astype(jnp.bfloat16)
+        copy = pltpu.make_async_copy(staged.at[rows], out_hbm.at[rows], sem.at[high])
+        copy.start()
+        copies.append(copy)
+    for copy in copies:
+        copy.wait()
 
 
 def body(values, long_filter, skip_gain):
     operands = (long_filter, values, *(jnp.asarray(t) for t in tables()))
-    convolved = pl.pallas_call(
+    blocks = pl.pallas_call(
         kernel,
-        out_shape=jax.ShapeDtypeStruct(values.shape, jnp.bfloat16),
+        out_shape=jax.ShapeDtypeStruct((2, N_DEV, 2 * HIGH, LOW), jnp.bfloat16),
         in_specs=[pl.BlockSpec(memory_space=pltpu.HBM)] * len(operands),
         out_specs=pl.BlockSpec(memory_space=pltpu.VMEM),
         scratch_shapes=[
@@ -247,8 +265,19 @@
             collective_id=0, has_side_effects=True, vmem_limit_bytes=107 * 2**19
         ),
     )(*operands)
-    direct = skip_gain[None, :] * values.astype(jnp.float32)
-    return (convolved.astype(jnp.float32) + direct).astype(jnp.bfloat16)
+    vmem = pl.BlockSpec(memory_space=pltpu.VMEM)
+    return pl.pallas_call(
+        finish,
+        out_shape=jax.ShapeDtypeStruct(values.shape, jnp.bfloat16),
+        in_specs=[vmem] * 3,
+        out_specs=pl.BlockSpec(memory_space=pltpu.HBM),
+        scratch_shapes=[
+            pltpu.VMEM((2, N_DEV * 2 * HIGH, LOW), jnp.float32),
+            pltpu.VMEM(values.shape, jnp.bfloat16),
+            pltpu.SemaphoreType.DMA((HIGH,)),
+        ],
+        compiler_params=pltpu.CompilerParams(vmem_limit_bytes=8 * 2**20),
+    )(blocks, values, skip_gain.reshape(1, values.shape[1]))
 
 
 def solution(mesh):

time: 35.9 us -> 35.9 us (level)
  other arithmetic: 0.79 us -> 0 us
  Pallas kernels: 35 us -> 35.7 us
    convert_element_type x1 -> x0, other arithmetic: 0.79 us -> none  [body(): return (convolved.astype(jnp.float32) + direct).astype(jnp.bfloat16)]
    pallas_call x1 -> x2, Pallas kernels: 35 us -> 35.7 us  [the longest x1 34.8 us: body(): pl.pallas_call(kernel, out_shape=jax.ShapeDtypeStruct((2, N_DEV, 2 * HIGH...]
where the time goes in v5:
time: 35.9 us; the launch traced here: 35.8 us
  Pallas kernels  35.7 us (99%)
    pallas_call x1, Pallas kernels, body(): pl.pallas_call(kernel, out_shape=jax.ShapeDtypeStruct((2, N_DEV, 2 * HIGH...  34.8 us
    pallas_call x1, Pallas kernels, body(): pl.pallas_call(finish, out_shape=jax.ShapeDtypeStruct(values.shape, jnp.b...  0.95 us

profile of v5, /device:TPU:6, one launch (start us, length us, event | category | flops | bytes accessed | tf_op | source)
XLA Modules:
  0.0 35.8 jit_solution(7463818273887067895)
XLA Ops:
  0.0 0.0 copy-start
  0.0 0.0 copy-start.1
  0.0 34.8 %shard_map.55.blocks_ref = bf16[2,32,16,128]{3,2,1,0:T(8,128)(2,1)S(1)} custom-call(bf16[1024,128]{1,0:T(8,128)(2,1)} %filter_hbm.1, bf16[1024,128]{1,0:T(8,128)(2,1)} %values_ref.1, bf16[1568,256]{1,0:T(8,128)(2,1)} %constant.4.clone.matrices_hbm, f32[544,128]{1,0:T(8,128)} %constant.5.clone.twists_hbm), custom_call_target="tpu_custom_call" | custom-call | tf_op jit(solution)/shard_map/pallas_call | solution.py:248
  34.8 0.0 copy-done
  34.8 0.0 copy-done.1
  34.8 0.9 %shard_map.56 = bf16[1024,128]{1,0:T(8,128)(2,1)} custom-call(bf16[2,32,16,128]{3,2,1,0:T(8,128)(2,1)S(1)} %shard_map.55.blocks_ref, bf16[1024,128]{1,0:T(8,128)(2,1)S(1)} %copy-done, f32[1,128]{1,0:T(1,128)S(1)} %bitcast.1), custom_call_target="tpu_custom_call" | custom-call | tf_op jit(solution)/shard_map/pallas_call | solution.py:269
Async XLA Ops:
  0.0 34.8 %copy-start = (bf16[1024,128]{1,0:T(8,128)(2,1)S(1)}, bf16[1024,128]{1,0:T(8,128)(2,1)}, u32[]{:S(2)}) copy-start(bf16[1024,128]{1,0:T(8,128)(2,1)} %values_ref.1) | copy-start | bytes 786436
  0.0 34.8 %copy-start.1 = (f32[128]{0:T(128)S(1)}, f32[128]{0:T(128)}, u32[]{:S(2)}) copy-start(f32[128]{0:T(128)} %param.7) | copy-start | bytes 1540

commit v6 on v5

--- a/solution.py
+++ b/solution.py
@@ -85,17 +85,16 @@
         pltpu.make_async_copy(source, target, load_sem.at[i])
         for i, (source, target) in enumerate(pairs)
     ]
-    loads[0].start()
-    for steps in FAR_FIRST:
-        pl.semaphore_signal(
-            barrier, inc=1, device_id={"context": partner(steps)}, device_id_type=MESH
-        )
     lane = lax.axis_index("tensor")
     sibling = lane + 1 - 2 * lax.rem(lane, 2)
     pl.semaphore_signal(
         barrier, inc=1, device_id={"tensor": sibling, "context": me}, device_id_type=MESH
     )
-    for load in loads[1:]:
+    for steps in FAR_FIRST:
+        pl.semaphore_signal(
+            barrier, inc=1, device_id={"context": partner(steps)}, device_id_type=MESH
+        )
+    for load in loads:
         load.start()
 
     rows = [0, 2 * K1, 2 * K1 + 2 * LOW, 2 * K1 + 4 * LOW, 2 * K1 + 4 * LOW + N1]

time: 35.9 us -> 35.9 us (level)
  no operation moved by 1% of the time
where the time goes in v6:
time: 35.9 us; the launch traced here: 35.7 us
  Pallas kernels  35.7 us (99%)
    pallas_call x1, Pallas kernels, body(): pl.pallas_call(kernel, out_shape=jax.ShapeDtypeStruct((2, N_DEV, 2 * HIGH...  34.7 us
    pallas_call x1, Pallas kernels, body(): pl.pallas_call(finish, out_shape=jax.ShapeDtypeStruct(values.shape, jnp.b...  0.95 us

profile of v6, /device:TPU:6, one launch (start us, length us, event | category | flops | bytes accessed | tf_op | source)
XLA Modules:
  0.0 35.7 jit_solution(13613166329863083319)
XLA Ops:
  0.0 0.0 copy-start
  0.0 0.0 copy-start.1
  0.0 34.7 %shard_map.55.blocks_ref = bf16[2,32,16,128]{3,2,1,0:T(8,128)(2,1)S(1)} custom-call(bf16[1024,128]{1,0:T(8,128)(2,1)} %filter_hbm.1, bf16[1024,128]{1,0:T(8,128)(2,1)} %values_ref.1, bf16[1568,256]{1,0:T(8,128)(2,1)} %constant.4.clone.matrices_hbm, f32[544,128]{1,0:T(8,128)} %constant.5.clone.twists_hbm), custom_call_target="tpu_custom_call" | custom-call | tf_op jit(solution)/shard_map/pallas_call | solution.py:247
  34.8 0.0 copy-done
  34.8 0.0 copy-done.1
  34.8 0.9 %shard_map.56 = bf16[1024,128]{1,0:T(8,128)(2,1)} custom-call(bf16[2,32,16,128]{3,2,1,0:T(8,128)(2,1)S(1)} %shard_map.55.blocks_ref, bf16[1024,128]{1,0:T(8,128)(2,1)S(1)} %copy-done, f32[1,128]{1,0:T(1,128)S(1)} %bitcast.1), custom_call_target="tpu_custom_call" | custom-call | tf_op jit(solution)/shard_map/pallas_call | solution.py:268
Async XLA Ops:
  0.0 34.8 %copy-start = (bf16[1024,128]{1,0:T(8,128)(2,1)S(1)}, bf16[1024,128]{1,0:T(8,128)(2,1)}, u32[]{:S(2)}) copy-start(bf16[1024,128]{1,0:T(8,128)(2,1)} %values_ref.1) | copy-start | bytes 786436
  0.0 34.8 %copy-start.1 = (f32[128]{0:T(128)S(1)}, f32[128]{0:T(128)}, u32[]{:S(2)}) copy-start(f32[128]{0:T(128)} %param.7) | copy-start | bytes 1540
